TPU v7x, 32 devices: a whole 2x2x4 slice. The times are simulated.
32 devices in a mesh: jobs: 2 (over x), seq: 16 (over z, y, core).
Axes of the slice: x: 2, y: 2, z: 4, core: 2. Of those that a mesh axis runs over, the one named last changes fastest.
Arguments:
- queries: bfloat16 [1024, 4096], P(('jobs', 'seq')), parts along dimension 0, may hold values from -12 to 12
- keys: bfloat16 [1024, 4096], P(('jobs', 'seq')), parts along dimension 0, may hold values from -6 to 6
- values: bfloat16 [1024, 4096], P(('jobs', 'seq')), parts along dimension 0, may hold values from -6 to 6
- live_counts: int32 [2, 16], P('jobs', 'seq'), parts along dimension 0, may hold values from 4 to 16, as said below
- merge_dest: int32 [2, 1024], P('jobs', 'seq'), parts along dimension 0, may hold values from 0 to 15, as said below
- latents: float32 [2, 1024, 64], P('jobs', 'seq'), parts along dimension 0, may hold values from -6 to 6
- guidance: float32 [2], P('jobs'), parts along dimension 0, may hold values from 3 to 6
- step_index: int32 [2], P('jobs'), parts along dimension 0, may hold values from 0 to 980
- out_weight: bfloat16 [4096, 64], replicated, may hold values from -0.09375 to 0.09375
Outputs:
- denoised: float32 [2, 1024, 64], P('jobs', 'seq'), parts along dimension 0
- merged_next: float32 [2, 256, 64], P('jobs', 'seq'), parts along dimension 0
There are 2 independent parts, one for each index of `jobs`. A program takes and returns all parts, laid end to end along the dimension named above; an argument that names none is the same for every part. Nothing has to cross between parts.
Inputs may be any that keep to these rules, and one draw needn't show every extreme that they name: `live_counts`: in every video some merge group has exactly 16 live slots. `merge_dest`: each token names a slot of its own merge group below that group's live count, and every live slot is named by at least one token.
All inputs are finite; a program needn't handle non-finite values.
Results may differ from a plain program's by a relative error of at most 0.0031.
Values may be sent and summed in bfloat16 or wider, within the bound.
A program may use at most 64 MiB of HBM per device.

v0:
```python
import math

import jax
import jax.numpy as jnp
from jax import lax
from jax.sharding import PartitionSpec as P

HEADS = 32
HD = 128
TIMESTEPS = 1000
STRIDE = 20


neg_big = -1e30
shift_value = 5.0


def sigma_of(step_value):
    frac = 1.0 - step_value / TIMESTEPS
    return shift_value * frac / (1.0 + (shift_value - 1.0) * frac)


def attend_branch(query_rows, key_rows, value_rows, key_live, score_scale):
    total_rows = query_rows.shape[0]
    block_rows = 512 if total_rows % 512 == 0 else total_rows

    def one_block(query_block):
        scores = (
            lax.dot_general(
                query_block, key_rows, (((1,), (1,)), ((), ())), preferred_element_type=jnp.float32
            )
            * score_scale
        )
        scores = jnp.where(key_live[None, :], scores, neg_big)
        row_top = jnp.max(scores, axis=-1, keepdims=True)
        weights = jnp.exp(scores - row_top)
        probabilities = (weights / jnp.sum(weights, axis=-1, keepdims=True)).astype(jnp.bfloat16)
        return jnp.dot(probabilities, value_rows, preferred_element_type=jnp.float32).astype(
            jnp.bfloat16
        )

    blocks = query_rows.reshape(total_rows // block_rows, block_rows, query_rows.shape[1])
    return lax.map(one_block, blocks).reshape(total_rows, query_rows.shape[1])


def local(
    queries, keys, values, live_counts, merge_dest, latents, guidance, step_index, out_weight
):
    groups = lax.axis_size("seq")
    device = lax.axis_index("seq")
    pair_count = groups // 2
    local_rows, columns = queries.shape
    cap_half = local_rows // 2
    videos = guidance.shape[0]
    feature_width = columns // videos
    per_device = columns // groups
    item_count = per_device // HD
    branch_slots = groups * cap_half
    score_scale = 1.0 / math.sqrt(HD)
    counts_all = lax.all_gather(live_counts, "seq", axis=1, tiled=True)
    query_in, key_in, value_in = (
        lax.all_to_all(queries, "seq", split_axis=1, concat_axis=0, tiled=True),
        lax.all_to_all(keys, "seq", split_axis=1, concat_axis=0, tiled=True),
        lax.all_to_all(values, "seq", split_axis=1, concat_axis=0, tiled=True),
    )
    count_grid = counts_all.reshape(videos, 2, pair_count).transpose(0, 2, 1)
    live_slots = (
        jnp.arange(cap_half, dtype=jnp.int32)[None, None, None, :] < count_grid[..., None]
    ).reshape(videos, branch_slots)
    guided_parts = []
    head_numbers = []
    for item_index in range(item_count):
        global_item = device * item_count + item_index
        video_index = global_item // HEADS
        key_live = live_slots[video_index]
        col_start = item_index * HD
        branch_outs = []
        for branch_no in range(2):
            row_start = branch_no * branch_slots
            branch_outs.append(
                attend_branch(
                    query_in[row_start : row_start + branch_slots, col_start : col_start + HD],
                    key_in[row_start : row_start + branch_slots, col_start : col_start + HD],
                    value_in[row_start : row_start + branch_slots, col_start : col_start + HD],
                    key_live,
                    score_scale,
                )
            )
        conditioned = branch_outs[0].astype(jnp.float32)
        uncond = branch_outs[1].astype(jnp.float32)
        guided_parts.append(
            (uncond + guidance[video_index] * (conditioned - uncond)).astype(jnp.bfloat16)
        )
        head_numbers.append(global_item % HEADS)
    stacked = jnp.concatenate(guided_parts, axis=1)
    ordered = (
        stacked.reshape(pair_count, 2, cap_half, per_device)
        .transpose(1, 0, 2, 3)
        .reshape(groups * cap_half, per_device)
    )
    mixed = lax.all_to_all(ordered, "seq", split_axis=0, concat_axis=1, tiled=True)
    merged = jnp.einsum(
        "jva,ac->vjc",
        mixed.reshape(cap_half, videos, feature_width),
        out_weight,
        preferred_element_type=jnp.float32,
    )
    onehot = (merge_dest[..., None] == jnp.arange(cap_half, dtype=jnp.int32)).astype(jnp.float32)
    velocity = jnp.einsum("vrj,vjc->vrc", onehot, merged, precision=lax.Precision.HIGHEST)
    step_value = step_index.astype(jnp.float32)
    sigma_now = sigma_of(step_value)
    sigma_next = sigma_of(step_value + float(STRIDE))
    denoised = latents - sigma_now[:, None, None] * velocity
    advanced = latents + (sigma_next - sigma_now)[:, None, None] * velocity
    slot_sums = jnp.einsum("vrj,vrc->vjc", onehot, advanced, precision=lax.Precision.HIGHEST)
    slot_tally = jnp.sum(onehot, axis=1)
    merged_next = slot_sums / jnp.maximum(slot_tally, 1.0)[..., None]
    return (denoised, merged_next)


def solution(mesh):
    placed = (
        P(("jobs", "seq"), None),
        P(("jobs", "seq"), None),
        P(("jobs", "seq"), None),
        P("jobs", "seq"),
        P("jobs", "seq"),
        P("jobs", "seq", None),
        P("jobs"),
        P("jobs"),
        P(),
    )
    return jax.shard_map(
        local,
        mesh=mesh,
        in_specs=placed,
        out_specs=(P("jobs", "seq", None), P("jobs", "seq", None)),
        check_vma=False,
    )
```

profile of v0, /device:TPU:0, one launch (start us, length us, event | category | flops | bytes accessed | tf_op | source)
XLA Modules:
  0.0 69.6 jit_solution(11512666287636155792)
XLA Ops:
  0.6 0.0 copy-start
  0.6 1.7 %copy.78 = bf16[4,16,8,256]{3,2,0,1:T(8,128)(2,1)} copy(bf16[4,16,8,256]{3,2,1,0:T(8,128)(2,1)} %bitcast.66) | data formatting | bytes 524288 | tf_op jit(solution)/shard_map/all_to_all | solution.py:62
  2.4 0.0 copy-start.1
  2.4 7.5 %all-to-all-start = ((bf16[32,16,256]{2,0,1:T(8,128)(2,1)}), bf16[32,16,256]{2,0,1:T(8,128)(2,1)S(1)}, u32[]{:S(2)}, u32[]{:S(2)}) async-start(bf16[32,16,256]{2,0,1:T(8,128)(2,1)} %bitcast.62), calls=%async_computation | async-start | bytes 524288 | tf_op jit(solution)/shard_map/all_to_all | solution.py:62
  9.9 0.0 copy-done.1
  9.9 0.7 %copy.77 = bf16[4,16,8,256]{3,2,0,1:T(8,128)(2,1)} copy(bf16[4,16,8,256]{3,2,1,0:T(8,128)(2,1)S(1)} %bitcast.67) | data formatting | bytes 524288 | tf_op jit(solution)/shard_map/all_to_all | solution.py:63
  10.6 9.3 %all-to-all-done = bf16[32,16,256]{2,0,1:T(8,128)(2,1)S(1)} async-done(((bf16[32,16,256]{2,0,1:T(8,128)(2,1)}), bf16[32,16,256]{2,0,1:T(8,128)(2,1)S(1)}, u32[]{:S(2)}, u32[]{:S(2)}) %all-to-all-start) | async-done | bytes 262176 | tf_op jit(solution)/shard_map/all_to_all | solution.py:62
  20.0 0.0 copy-start.2
  20.0 3.7 %all-to-all-start.1 = ((bf16[32,16,256]{2,0,1:T(8,128)(2,1)}), bf16[32,16,256]{2,0,1:T(8,128)(2,1)S(1)}, u32[]{:S(2)}, u32[]{:S(2)}) async-start(bf16[32,16,256]{2,0,1:T(8,128)(2,1)} %bitcast.61), calls=%async_computation.1 | async-start | bytes 524288 | tf_op jit(solution)/shard_map/all_to_all | solution.py:63
  24.3 0.0 copy-start.5
  24.3 0.6 copy-done.5
  24.9 0.6 dynamic-slice.4
  25.5 0.7 bitcast_dynamic-update-slice_fusion
  26.2 12.4 %all-reduce = s32[16]{0:T(128)S(1)} all-reduce(s32[16]{0:T(128)S(1)} %bitcast_dynamic-update-slice_fusion), channel_id=1, replica_groups=mesh['jobs'=2,'seq'=16] {'seq'}, use_global_device_ids=true, to_apply=%add | all-reduce | flops 16 | bytes 128
  38.6 0.1 reshape.221
  38.7 0.1 copy.42
  38.8 0.1 iota_compare_fusion.4
  38.8 0.1 lt.36
  38.9 0.0 copy-done.2
  38.9 0.7 %copy.76 = bf16[4,16,8,256]{3,2,0,1:T(8,128)(2,1)} copy(bf16[4,16,8,256]{3,2,1,0:T(8,128)(2,1)S(1)} %bitcast.68) | data formatting | bytes 524288 | tf_op jit(solution)/shard_map/all_to_all | solution.py:64
  40.3 0.0 all-to-all-done.1
  40.3 3.5 %all-to-all-start.2 = ((bf16[32,16,256]{2,0,1:T(8,128)(2,1)}), bf16[32,16,256]{2,0,1:T(8,128)(2,1)S(1)}, u32[]{:S(2)}, u32[]{:S(2)}) async-start(bf16[32,16,256]{2,0,1:T(8,128)(2,1)} %bitcast.60), calls=%async_computation.2 | async-start | bytes 524288 | tf_op jit(solution)/shard_map/all_to_all | solution.py:64
  43.9 0.2 fusion.35
  44.1 0.2 fusion.36
  44.3 0.1 fusion.8
  44.4 0.2 fusion.37
  44.6 0.2 fusion.38
  44.8 9.1 %all-to-all-done.2 = bf16[32,16,256]{2,0,1:T(8,128)(2,1)S(1)} async-done(((bf16[32,16,256]{2,0,1:T(8,128)(2,1)}), bf16[32,16,256]{2,0,1:T(8,128)(2,1)S(1)}, u32[]{:S(2)}, u32[]{:S(2)}) %all-to-all-start.2) | async-done | bytes 262176 | tf_op jit(solution)/shard_map/all_to_all | solution.py:64
  53.9 0.2 convolution_convert_fusion
  54.1 0.1 fusion.7
  54.2 0.2 convolution_convert_fusion.1
  54.4 0.1 fusion.6
  54.5 0.2 convolution_convert_fusion.2
  54.8 0.1 fusion.5
  54.8 0.2 convolution_convert_fusion.3
  55.1 0.1 fusion.11
  55.2 0.7 pad_maximum_fusion
  55.8 3.5 %all-to-all-start.3 = ((bf16[16,16,256]{2,1,0:T(8,128)(2,1)}), bf16[16,16,256]{2,1,0:T(8,128)(2,1)S(1)}, u32[]{:S(2)}, u32[]{:S(2)}) async-start(bf16[16,16,256]{2,1,0:T(8,128)(2,1)} %bitcast.23), calls=%async_computation.3 | async-start | bytes 262144 | tf_op jit(solution)/shard_map/all_to_all | solution.py:101
  59.3 0.0 copy-start.4
  59.3 0.6 copy-done.4
  60.0 0.1 convert_reduce_fusion
  60.9 6.4 %all-to-all-done.3 = bf16[16,16,256]{2,1,0:T(8,128)(2,1)S(1)} async-done(((bf16[16,16,256]{2,1,0:T(8,128)(2,1)}), bf16[16,16,256]{2,1,0:T(8,128)(2,1)S(1)}, u32[]{:S(2)}, u32[]{:S(2)}) %all-to-all-start.3) | async-done | bytes 131104 | tf_op jit(solution)/shard_map/all_to_all | solution.py:101
  67.2 0.0 copy-done
  67.2 0.0 copy-start.3
  67.3 0.2 fusion.39
  67.5 0.5 copy-done.3
  68.0 0.8 %bitcast_subtract_fusion = (f32[1,64,64]{2,1,0:T(8,128)}, f32[64,64]{1,0:T(8,128)S(1)}) fusion(f32[1,64,64]{2,1,0:T(8,128)S(1)} %copy-done.3, f32[]{:T(128)} %bitcast, f32[16,64]{1,0:T(8,128)S(1)} %fusion.39, s32[64]{0:T(128)S(1)} %bitcast.86), kind=kOutput, calls=%fused_computation.52 | convolution fusion | flops 795648 | bytes 53508 | tf_op jit(solution)/shard_map/vrj,vjc->vrc/dot_general | solution.py:109
  68.8 0.7 %fusion.4 = f32[1,16,64]{2,1,0:T(8,128)} fusion(f32[1,64,64]{2,1,0:T(8,128)S(1)} %copy-done.3, f32[64,64]{1,0:T(8,128)S(1)} %get-tuple-element.65, f32[]{:T(128)} %bitcast.27, f32[16]{0:T(128)S(1)} %broadcast_maximum_fusion, s32[64]{0:T(128)S(1)} %bitcast.87), kind=kOutput, calls=%fused_computation.13 | convolution fusion | flops 796672 | bytes 37188 | tf_op jit(solution)/shard_map/vrj,vrc->vjc/dot_general | solution.py:115
  (3 shorter events, 0.0 us)
Async XLA Ops:
  0.6 66.6 %copy-start = (bf16[4096,64]{0,1:T(8,128)(2,1)S(1)}, bf16[4096,64]{0,1:T(8,128)(2,1)}, u32[]{:S(2)}) copy-start(bf16[4096,64]{0,1:T(8,128)(2,1)} %param.17) | copy-start | bytes 1572868
  2.4 7.5 %copy-start.1 = (bf16[32,4096]{1,0:T(8,128)(2,1)S(1)}, bf16[32,4096]{1,0:T(8,128)(2,1)}, u32[]{:S(2)}) copy-start(bf16[32,4096]{1,0:T(8,128)(2,1)} %param.10) | copy-start | bytes 786436
  2.4 17.6 %all-to-all-start = ((bf16[32,16,256]{2,0,1:T(8,128)(2,1)}), bf16[32,16,256]{2,0,1:T(8,128)(2,1)S(1)}, u32[]{:S(2)}, u32[]{:S(2)}) async-start(bf16[32,16,256]{2,0,1:T(8,128)(2,1)} %bitcast.62), calls=%async_computation | async-start | bytes 524288 | tf_op jit(solution)/shard_map/all_to_all | solution.py:62
  20.0 19.0 %copy-start.2 = (bf16[32,4096]{1,0:T(8,128)(2,1)S(1)}, bf16[32,4096]{1,0:T(8,128)(2,1)}, u32[]{:S(2)}) copy-start(bf16[32,4096]{1,0:T(8,128)(2,1)} %param.11) | copy-start | bytes 786436
  20.0 20.4 %all-to-all-start.1 = ((bf16[32,16,256]{2,0,1:T(8,128)(2,1)}), bf16[32,16,256]{2,0,1:T(8,128)(2,1)S(1)}, u32[]{:S(2)}, u32[]{:S(2)}) async-start(bf16[32,16,256]{2,0,1:T(8,128)(2,1)} %bitcast.61), calls=%async_computation.1 | async-start | bytes 524288 | tf_op jit(solution)/shard_map/all_to_all | solution.py:63
  24.3 0.7 copy-start.5
  40.3 13.6 %all-to-all-start.2 = ((bf16[32,16,256]{2,0,1:T(8,128)(2,1)}), bf16[32,16,256]{2,0,1:T(8,128)(2,1)S(1)}, u32[]{:S(2)}, u32[]{:S(2)}) async-start(bf16[32,16,256]{2,0,1:T(8,128)(2,1)} %bitcast.60), calls=%async_computation.2 | async-start | bytes 524288 | tf_op jit(solution)/shard_map/all_to_all | solution.py:64
  55.8 11.4 %all-to-all-start.3 = ((bf16[16,16,256]{2,1,0:T(8,128)(2,1)}), bf16[16,16,256]{2,1,0:T(8,128)(2,1)S(1)}, u32[]{:S(2)}, u32[]{:S(2)}) async-start(bf16[16,16,256]{2,1,0:T(8,128)(2,1)} %bitcast.23), calls=%async_computation.3 | async-start | bytes 262144 | tf_op jit(solution)/shard_map/all_to_all | solution.py:101
  59.3 0.7 copy-start.4
  67.2 0.8 %copy-start.3 = (f32[1,64,64]{2,1,0:T(8,128)S(1)}, f32[1,64,64]{2,1,0:T(8,128)}, u32[]{:S(2)}) copy-start(f32[1,64,64]{2,1,0:T(8,128)} %param.14) | copy-start | bytes 49156
where the time goes:
time: 70.2 us; the launch traced here: 69.6 us
  waiting for transfers between devices  24.7 us (35%)
  starting transfers between devices  18.2 us (26%)
  blocking collectives  12.4 us (18%)
  local copies, waits for them, and re-layouts  6.53 us (9%)
  matrix products  3.65 us (5%)
  between operations  2.84 us (4%)
  other arithmetic  1.2 us (2%)
    unnamed x1, blocking collectives  12.4 us
    all_to_all x1, waiting for transfers between devices, local(): lax.all_to_all(queries, 'seq', split_axis=1, concat_axis=0, tiled=True)  9.32 us
    all_to_all x1, waiting for transfers between devices, local(): lax.all_to_all(values, 'seq', split_axis=1, concat_axis=0, tiled=True)  9.05 us
    all_to_all x1, starting transfers between devices, local(): lax.all_to_all(queries, 'seq', split_axis=1, concat_axis=0, tiled=True)  7.52 us
    all_to_all x1, waiting for transfers between devices, local(): lax.all_to_all(ordered, 'seq', split_axis=0, concat_axis=1, tiled=True)  6.37 us
    all_to_all x1, starting transfers between devices, local(): lax.all_to_all(keys, 'seq', split_axis=1, concat_axis=0, tiled=True)  3.66 us
    all_to_all x1, starting transfers between devices, local(): lax.all_to_all(values, 'seq', split_axis=1, concat_axis=0, tiled=True)  3.54 us
    all_to_all x1, starting transfers between devices, local(): lax.all_to_all(ordered, 'seq', split_axis=0, concat_axis=1, tiled=True)  3.51 us
  transfers between devices with their start and end apart: 4, of which 3 were waited for; matrix products, arithmetic and copies ran while one was open for 6% of the time, Pallas kernels for 0%

commit v1 on v0

v1 whole, which is shorter than its diff:
```python
import functools
import math

import jax
import jax.numpy as jnp
from jax import lax
from jax.experimental import pallas as pl
from jax.experimental.pallas import tpu as pltpu
from jax.sharding import PartitionSpec as P

HEADS = 32
HD = 128
TIMESTEPS = 1000
STRIDE = 20
NEG_BIG = -1e30
SHIFT = 5.0
MESH = pl.DeviceIdType.MESH


def sigma_of(step_value):
    frac = 1.0 - step_value / TIMESTEPS
    return SHIFT * frac / (1.0 + (SHIFT - 1.0) * frac)


def sweep(first, last, body):
    if last - first <= 16:
        for index in range(first, last):
            body(index)
    else:

        def step(index, carry):
            body(index)
            return carry

        lax.fori_loop(first, last, step, 0)


def kernel(
    n,
    items,
    videos,
    query_hbm,
    key_hbm,
    value_hbm,
    count_hbm,
    dest_hbm,
    latent_hbm,
    guidance_hbm,
    step_hbm,
    weight_hbm,
    denoised_ref,
    merged_ref,
    heads_buf,
    count_own,
    count_buf,
    weight_own,
    weight_twice,
    latent_buf,
    dest_buf,
    count_smem,
    guidance_smem,
    step_smem,
    total,
    stage,
    parts,
    barrier_like_sems,
    small_sems,
    head_recv,
    send_sems,
):
    half = n // 2
    me = lax.axis_index("seq")
    branch = me // half
    rank = me % half
    base = branch * half
    rows = query_hbm.shape[0]
    cap = rows // 2
    keys_total = half * rows
    channels = weight_hbm.shape[1]
    scale = 1.0 / math.sqrt(HD)
    sources = (query_hbm, key_hbm, value_hbm)

    barrier = pltpu.get_barrier_semaphore()

    def greet(p):
        pl.semaphore_signal(
            barrier, inc=1, device_id={"seq": (me + p) % n}, device_id_type=MESH
        )

    sweep(1, n, greet)

    count_copy = pltpu.make_async_copy(count_hbm, count_smem, small_sems.at[0])
    count_copy.start()
    head_row = pl.multiple_of(((rank * items) % HEADS) * HD, HD)
    small_copies = [
        pltpu.make_async_copy(guidance_hbm, guidance_smem, small_sems.at[1]),
        pltpu.make_async_copy(step_hbm, step_smem, small_sems.at[2]),
        pltpu.make_async_copy(
            weight_hbm.at[pl.ds(head_row, items * HD)], weight_own, small_sems.at[3]
        ),
        pltpu.make_async_copy(latent_hbm, latent_buf, small_sems.at[4]),
        pltpu.make_async_copy(dest_hbm, dest_buf, small_sems.at[5]),
    ]
    for copy in small_copies:
        copy.start()
    row_at = pl.multiple_of(rank * rows, rows)
    for item in range(items):
        for which in range(3):
            column = pl.multiple_of((rank * items + item) * HD, HD)
            pltpu.make_async_copy(
                sources[which].at[:, pl.ds(column, HD)],
                heads_buf.at[item, which, pl.ds(row_at, rows)],
                head_recv.at[item],
            ).start()

    count_copy.wait()
    count_own[...] = jnp.full(count_own.shape, count_smem[0, 0], jnp.int32) if videos == 1 else (
        jnp.concatenate(
            [jnp.full((1, 128), count_smem[v, 0], jnp.int32) for v in range(videos)], axis=0
        )
    )
    pltpu.make_async_copy(count_own, count_buf.at[me], barrier_like_sems.at[0]).start()

    pl.semaphore_wait(barrier, n - 1)

    def send_count(p):
        pltpu.make_async_remote_copy(
            src_ref=count_own,
            dst_ref=count_buf.at[me],
            send_sem=send_sems.at[0],
            recv_sem=barrier_like_sems.at[0],
            device_id={"seq": (me + p) % n},
            device_id_type=MESH,
        ).start()

    for item in range(items):

        def send_heads(p):
            peer = (rank + p) % half
            column = pl.multiple_of((peer * items + item) * HD, HD)
            for which in range(3):
                pltpu.make_async_remote_copy(
                    src_ref=sources[which].at[:, pl.ds(column, HD)],
                    dst_ref=heads_buf.at[item, which, pl.ds(row_at, rows)],
                    send_sem=send_sems.at[1],
                    recv_sem=head_recv.at[item],
                    device_id={"seq": base + peer},
                    device_id_type=MESH,
                ).start()

        sweep(1, half, send_heads)
        if item == 0:
            sweep(1, n, send_count)

    for copy in small_copies:
        copy.wait()
    weight_twice[...] = jnp.concatenate([weight_own[...], weight_own[...]], axis=1)
    tokens = latent_buf.shape[1]
    slot_hots = []
    latent_sums = []
    for v in range(videos):
        hot = lax.broadcasted_iota(jnp.int32, (cap, tokens), 0) == dest_buf[pl.ds(v, 1), :]
        hot = hot.astype(jnp.float32)
        slot_hots.append(hot)
        latent_sums.append(
            jnp.dot(
                hot,
                latent_buf[v],
                precision=lax.Precision.HIGHEST,
                preferred_element_type=jnp.float32,
            )
        )

    pltpu.make_async_copy(count_buf, count_buf, barrier_like_sems.at[0]).wait()
    video = (rank * items) // HEADS
    lane = lax.broadcasted_iota(jnp.int32, (1, keys_total), 1)
    group_of = ((lane % rows) // cap) * half + lane // rows
    place_of = lane % cap

    def count_step(m, held):
        row = count_buf[m][0:1]
        for v in range(1, videos):
            row = jnp.where(video == v, count_buf[m][v : v + 1], row)
        wide = jnp.concatenate([row] * (keys_total // 128), axis=1)
        return jnp.where(group_of == m, wide, held)

    held = jnp.zeros((1, keys_total), jnp.int32)
    if n <= 16:
        for m in range(n):
            held = count_step(m, held)
    else:
        held = lax.fori_loop(0, n, count_step, held)
    live = place_of < held

    block = min(keys_total, 256)

    for item in range(items):
        pltpu.make_async_copy(heads_buf.at[item], heads_buf.at[item], head_recv.at[item]).wait()

        def attend(index):
            at = pl.ds(pl.multiple_of(index * block, block), block)
            scores = (
                lax.dot_general(
                    heads_buf[item, 0, at, :],
                    heads_buf[item, 1],
                    (((1,), (1,)), ((), ())),
                    preferred_element_type=jnp.float32,
                )
                * scale
            )
            scores = jnp.where(live, scores, NEG_BIG)
            weights = jnp.exp(scores - jnp.max(scores, axis=-1, keepdims=True))
            inverse = 1.0 / jnp.sum(weights, axis=-1, keepdims=True)
            probs = (weights * inverse).astype(jnp.bfloat16)
            attended = jnp.dot(
                probs, heads_buf[item, 2], preferred_element_type=jnp.float32
            ).astype(jnp.bfloat16)
            term = jnp.dot(
                attended,
                weight_twice[item * HD : (item + 1) * HD, :],
                preferred_element_type=jnp.float32,
            )
            if item == 0:
                total[at, :] = term
            else:
                total[at, :] += term

        if keys_total == block:
            attend(0)
        else:

            def attend_step(index, carry):
                attend(index)
                return carry

            lax.fori_loop(0, keys_total // block, attend_step, 0)

    gain = guidance_smem[0]
    for v in range(1, videos):
        gain = jnp.where(video == v, guidance_smem[v], gain)
    gain = jnp.where(branch == 0, gain, 1.0 - gain)
    both = total[...].reshape(half, 2, 2, cap // 2, 2 * channels)
    left = lax.broadcasted_iota(jnp.int32, (half, 2, cap // 2, 2 * channels), 3) < channels
    stage[...] = jnp.where(left, both[:, :, 0], both[:, :, 1]) * gain

    pltpu.make_async_copy(
        stage.at[rank, branch], parts.at[me], barrier_like_sems.at[1]
    ).start()

    def send_part(p):
        peer = (me + p) % n
        pltpu.make_async_remote_copy(
            src_ref=stage.at[peer % half, peer // half],
            dst_ref=parts.at[me],
            send_sem=send_sems.at[2],
            recv_sem=barrier_like_sems.at[1],
            device_id={"seq": peer},
            device_id_type=MESH,
        ).start()

    sweep(1, n, send_part)
    pltpu.make_async_copy(parts, parts, barrier_like_sems.at[1]).wait()

    span = half // videos
    for v in range(videos):
        summed = jnp.sum(parts[v * span : (v + 1) * span], axis=0) + jnp.sum(
            parts[half + v * span : half + (v + 1) * span], axis=0
        )
        merged = jnp.concatenate([summed[:, :channels], summed[:, channels:]], axis=0)
        velocity = lax.dot_general(
            slot_hots[v],
            merged,
            (((0,), (0,)), ((), ())),
            precision=lax.Precision.HIGHEST,
            preferred_element_type=jnp.float32,
        )
        step_value = jnp.full((1, channels), step_smem[v], jnp.int32).astype(jnp.float32)
        sigma_now = sigma_of(step_value)
        sigma_next = sigma_of(step_value + float(STRIDE))
        denoised_ref[v] = latent_buf[v] - sigma_now * velocity
        tally = jnp.sum(slot_hots[v], axis=1, keepdims=True)
        merged_ref[v] = (
            latent_sums[v] + tally * ((sigma_next - sigma_now) * merged)
        ) / jnp.maximum(tally, 1.0)

    pltpu.make_async_copy(
        count_buf.at[pl.ds(0, n - 1)], count_buf.at[pl.ds(0, n - 1)], send_sems.at[0]
    ).wait()
    sent = heads_buf.at[:, :, pl.ds(0, (half - 1) * rows)]
    pltpu.make_async_copy(sent, sent, send_sems.at[1]).wait()
    pltpu.make_async_copy(
        parts.at[pl.ds(0, n - 1)], parts.at[pl.ds(0, n - 1)], send_sems.at[2]
    ).wait()


def local(
    queries, keys, values, live_counts, merge_dest, latents, guidance, step_index, out_weight
):
    n = lax.axis_size("seq")
    half = n // 2
    rows, columns = queries.shape
    videos, tokens, channels = latents.shape
    items = columns // HD // half
    cap = rows // 2
    anywhere = pl.BlockSpec(memory_space=pl.ANY)
    inside = pl.BlockSpec(memory_space=pltpu.VMEM)
    denoised, merged_next = pl.pallas_call(
        functools.partial(kernel, n, items, videos),
        out_shape=(
            jax.ShapeDtypeStruct((videos, tokens, channels), jnp.float32),
            jax.ShapeDtypeStruct((videos, cap, channels), jnp.float32),
        ),
        in_specs=[anywhere] * 9,
        out_specs=(inside, inside),
        scratch_shapes=[
            pltpu.VMEM((items, 3, half * rows, HD), jnp.bfloat16),
            pltpu.VMEM((videos, 128), jnp.int32),
            pltpu.VMEM((n, videos, 128), jnp.int32),
            pltpu.VMEM((items * HD, channels), jnp.bfloat16),
            pltpu.VMEM((items * HD, 2 * channels), jnp.bfloat16),
            pltpu.VMEM((videos, tokens, channels), jnp.float32),
            pltpu.VMEM((videos, tokens), jnp.int32),
            pltpu.SMEM((videos, 1), jnp.int32),
            pltpu.SMEM((videos,), jnp.float32),
            pltpu.SMEM((videos,), jnp.int32),
            pltpu.VMEM((half * rows, 2 * channels), jnp.float32),
            pltpu.VMEM((half, 2, cap // 2, 2 * channels), jnp.float32),
            pltpu.VMEM((n, cap // 2, 2 * channels), jnp.float32),
            pltpu.SemaphoreType.DMA((2,)),
            pltpu.SemaphoreType.DMA((6,)),
            pltpu.SemaphoreType.DMA((items,)),
            pltpu.SemaphoreType.DMA((3,)),
        ],
        compiler_params=pltpu.CompilerParams(
            collective_id=0, has_side_effects=True, vmem_limit_bytes=48 * 1024 * 1024
        ),
    )(
        queries,
        keys,
        values,
        live_counts,
        merge_dest,
        latents,
        guidance,
        step_index,
        out_weight,
    )
    return denoised, merged_next


def solution(mesh):
    placed = (
        P(("jobs", "seq"), None),
        P(("jobs", "seq"), None),
        P(("jobs", "seq"), None),
        P("jobs", "seq"),
        P("jobs", "seq"),
        P("jobs", "seq", None),
        P("jobs"),
        P("jobs"),
        P(),
    )
    return jax.shard_map(
        local,
        mesh=mesh,
        in_specs=placed,
        out_specs=(P("jobs", "seq", None), P("jobs", "seq", None)),
        check_vma=False,
    )
```

time: 70.2 us -> 26.9 us (0.38)
  waiting for transfers between devices: 24.7 us -> 0 us
  Pallas kernels: 0 us -> 21.2 us
  starting transfers between devices: 18.2 us -> 0 us
  blocking collectives: 12.4 us -> 0 us
  local copies, waits for them, and re-layouts: 6.53 us -> 2.82 us
  matrix products: 3.65 us -> 0 us
  other arithmetic: 1.2 us -> 0 us
    all_to_all x4 -> x0, waiting for transfers between devices: 24.7 us -> none  [the longest x1 9.32 us: local(): lax.all_to_all(queries, 'seq', split_axis=1, concat_axis=0, tiled=True)]
    pallas_call x0 -> x1, Pallas kernels: none -> 21.2 us  [local(): pl.pallas_call(functools.partial(kernel, n, items, videos), out_shape=(ja...]
    all_to_all x4 -> x0, starting transfers between devices: 18.2 us -> none  [the longest x1 7.52 us: local(): lax.all_to_all(queries, 'seq', split_axis=1, concat_axis=0, tiled=True)]
    unnamed x1 -> x0, blocking collectives: 12.4 us -> none
    dot_general x11 -> x0, matrix products: 3.65 us -> none  [the longest x4 0.96 us: one_block(): jnp.dot(probabilities, value_rows, preferred_element_type=jnp.float32)]
    all_to_all x3 -> x0, local copies, waits for them, and re-layouts: 3.18 us -> none  [the longest x1 1.73 us: local(): lax.all_to_all(queries, 'seq', split_axis=1, concat_axis=0, tiled=True)]
    unnamed x15 -> x13, local copies, waits for them, and re-layouts: 3.08 us -> 2.82 us
  transfers between devices with their start and end apart: 4 -> 0, of which waited for: 3 -> 0; matrix products, arithmetic and copies ran while one was open for 6% -> 0% of each run, Pallas kernels for 0% -> 0%
where the time goes in v1:
time: 26.9 us; the launch traced here: 26.7 us
  Pallas kernels  21.2 us (79%)
  local copies, waits for them, and re-layouts  2.82 us (10%)
  between operations  2.66 us (10%)
    pallas_call x1, Pallas kernels, local(): pl.pallas_call(functools.partial(kernel, n, items, videos), out_shape=(ja...  21.2 us
    unnamed x13, local copies, waits for them, and re-layouts  2.82 us

profile of v1, /device:TPU:0, one launch (start us, length us, event | category | flops | bytes accessed | tf_op | source)
XLA Modules:
  0.0 26.7 jit_solution(17508383403036566623)
XLA Ops:
  2.6 0.0 copy-start
  2.6 0.0 copy-start.1
  2.6 0.0 copy-start.2
  2.6 0.0 copy-start.3
  2.6 0.0 copy-start.4
  2.6 1.6 %copy.11.weight_hbm = bf16[4096,64]{1,0:T(8,128)(2,1)S(1)} copy(bf16[4096,64]{0,1:T(8,128)(2,1)} %param.17) | data formatting | bytes 1048576 | tf_op args[8]
  4.2 0.0 copy-done
  4.2 0.0 copy-done.1
  4.2 0.0 copy-done.2
  4.2 0.0 copy-done.3
  4.2 0.0 copy-done.4
  4.3 21.2 %shard_map.104 = (f32[1,64,64]{2,1,0:T(8,128)S(1)}, f32[1,16,64]{2,1,0:T(8,128)S(1)}) custom-call(bf16[32,4096]{1,0:T(8,128)(2,1)S(1)} %copy-done, bf16[32,4096]{1,0:T(8,128)(2,1)S(1)} %copy-done.1, bf16[32,4096]{1,0:T(8,128)(2,1)S(1)} %copy-done.2, s32[1,1]{1,0:T(1,128)S(6)} %copy.14.count_hbm, s32[1,64]{1,0:T(1,128)S(1)} %copy-done.4, ...), custom_call_target="tpu_custom_call" | custom-call | tf_op jit(solution)/shard_map/pallas_call | solution.py:307
  25.5 0.6 %copy.17 = f32[1,64,64]{2,1,0:T(8,128)} copy(f32[1,64,64]{2,1,0:T(8,128)S(1)} %get-tuple-element.4) | data formatting | bytes 32768
  26.1 0.6 %copy.18 = f32[1,16,64]{2,1,0:T(8,128)} copy(f32[1,16,64]{2,1,0:T(8,128)S(1)} %get-tuple-element.5) | data formatting | bytes 8192
Async XLA Ops:
  2.6 1.6 %copy-start = (bf16[32,4096]{1,0:T(8,128)(2,1)S(1)}, bf16[32,4096]{1,0:T(8,128)(2,1)}, u32[]{:S(2)}) copy-start(bf16[32,4096]{1,0:T(8,128)(2,1)} %query_hbm.1) | copy-start | bytes 786436
  2.6 1.6 %copy-start.1 = (bf16[32,4096]{1,0:T(8,128)(2,1)S(1)}, bf16[32,4096]{1,0:T(8,128)(2,1)}, u32[]{:S(2)}) copy-start(bf16[32,4096]{1,0:T(8,128)(2,1)} %key_hbm.1) | copy-start | bytes 786436
  2.6 1.6 %copy-start.2 = (bf16[32,4096]{1,0:T(8,128)(2,1)S(1)}, bf16[32,4096]{1,0:T(8,128)(2,1)}, u32[]{:S(2)}) copy-start(bf16[32,4096]{1,0:T(8,128)(2,1)} %value_hbm.1) | copy-start | bytes 786436
  2.6 1.6 %copy-start.3 = (f32[1,64,64]{2,1,0:T(8,128)S(1)}, f32[1,64,64]{2,1,0:T(8,128)}, u32[]{:S(2)}) copy-start(f32[1,64,64]{2,1,0:T(8,128)} %latent_hbm.1) | copy-start | bytes 49156
  2.6 1.6 %copy-start.4 = (s32[1,64]{1,0:T(1,128)S(1)}, s32[1,64]{1,0:T(1,128)}, u32[]{:S(2)}) copy-start(s32[1,64]{1,0:T(1,128)} %dest_hbm.1) | copy-start | bytes 772
